TPU v7x, 128 devices: a whole 4x4x4 slice. The times are simulated.
128 devices in a mesh: dp: 4 (over y_hi, core), expert: 32 (over x, y_lo, z).
Axes of the slice: x: 4, y: 4 (y_hi: 2, y_lo: 2; y = y_hi * 2 + y_lo), z: 4, core: 2. Of those that a mesh axis runs over, the one named last changes fastest.
Arguments:
- tokens: bfloat16 [16384, 2048], P(('dp', 'expert')), may hold values from -6 to 6
- routes: int32 [16384, 6], P(('dp', 'expert')), may hold values from 0 to 63, all different within a row; in each aligned block of 128 rows (0 to 127, 128 to 255, ...) at most 16 rows name the same one
- gates: bfloat16 [16384, 6], P(('dp', 'expert')), may hold values from 0.099609375 to 1
- out_grad: bfloat16 [16384, 2048], P(('dp', 'expert')), may hold values from -3 to 3
- expert_gate_up: bfloat16 [64, 2048, 1408], P('expert'), may hold values from -0.125 to 0.125
- expert_down: bfloat16 [64, 704, 2048], P('expert'), may hold values from -0.21875 to 0.21875
- moving_slot: int32 [32], replicated, may hold values from 0 to 1
Outputs:
- mixed: bfloat16 [16384, 2048], P(('dp', 'expert'))
- token_grad: bfloat16 [16384, 2048], P(('dp', 'expert'))
- gate_up_grad: bfloat16 [64, 2048, 1408], P('expert', 'dp')
- down_grad: bfloat16 [64, 704, 2048], P('expert', None, 'dp')
Inputs may be any that keep to these rules, and one draw needn't show every extreme that they name: `routes`: each row names 6 different experts; among the rows of one device no expert is named more than 16 times, a bound that some block reaches.
All inputs are finite; a program needn't handle non-finite values.
Results may differ from a plain program's by a relative error of at most 0.012.
Values may be sent and summed in bfloat16 or wider, within the bound.
A program may use at most 192 MiB of HBM per device.

v0:
```python
import jax
import jax.numpy as jnp
from jax import lax
from jax.sharding import PartitionSpec as P


def from_partner(value, axis, bit):
    mask = 2**bit
    pairs = [(source, source ^ mask) for source in range(lax.axis_size(axis))]
    return lax.ppermute(value, axis, pairs)


def lookup(table, indices, count):
    match_grid = indices[:, None] == jnp.arange(count, dtype=jnp.int32)[None, :]
    return jnp.sum(jnp.where(match_grid, table[None, :], 0), axis=1)


def expert_block(recv_rows, scaled_cot, gate_up_local, down_local, hidden_width):
    projected = jnp.einsum(
        "snd,sdf->snf", recv_rows, gate_up_local, preferred_element_type=jnp.float32
    )
    pre_gate = projected[..., :hidden_width]
    pre_up = projected[..., hidden_width:]
    sigmoid_gate = jax.nn.sigmoid(pre_gate)
    activated = pre_gate * sigmoid_gate
    hidden = (activated * pre_up).astype(jnp.bfloat16)
    expert_out = jnp.einsum(
        "snf,sfd->snd", hidden, down_local, preferred_element_type=jnp.float32
    ).astype(jnp.bfloat16)
    hidden_grad = jnp.einsum(
        "snd,sfd->snf", scaled_cot, down_local, preferred_element_type=jnp.float32
    )
    grad_gate = hidden_grad * pre_up * sigmoid_gate * (1.0 + pre_gate * (1.0 - sigmoid_gate))
    grad_up = hidden_grad * activated
    pre_grad = jnp.concatenate([grad_gate, grad_up], axis=2).astype(jnp.bfloat16)
    row_grad = jnp.einsum(
        "snf,sdf->snd", pre_grad, gate_up_local, preferred_element_type=jnp.float32
    ).astype(jnp.bfloat16)
    down_part = jnp.einsum("snf,snd->sfd", hidden, scaled_cot, preferred_element_type=jnp.float32)
    gate_up_part = jnp.einsum(
        "snd,snf->sdf", recv_rows, pre_grad, preferred_element_type=jnp.float32
    )
    return (expert_out, row_grad, gate_up_part, down_part)


def on_device(tokens, routes, gates, out_grad, expert_gate_up, expert_down, moving_slot):
    host_count = lax.axis_size("expert")
    half_axis = host_count // 2
    pair_bit = host_count.bit_length() - 2
    own_index = lax.axis_index("expert")
    exp_local = expert_gate_up.shape[0]
    hidden_width = expert_down.shape[1]
    width = tokens.shape[1]
    rows_local, top_count = routes.shape
    expert_count = exp_local * host_count
    capacity = 4 * rows_local * top_count // (3 * expert_count)
    pair_count = rows_local * top_count
    total_slots = exp_local * host_count * capacity
    own_moving = moving_slot[own_index]
    outgoing = (
        lax.dynamic_index_in_dim(expert_gate_up, own_moving, 0, keepdims=False),
        lax.dynamic_index_in_dim(expert_down, own_moving, 0, keepdims=False),
    )
    got_gate_up, got_down = from_partner((outgoing[0], outgoing[1]), "expert", pair_bit)
    gate_up_local = lax.dynamic_update_index_in_dim(expert_gate_up, got_gate_up, own_moving, 0)
    down_local = lax.dynamic_update_index_in_dim(expert_down, got_down, own_moving, 0)
    flat_routes = routes.reshape(-1)
    home_host = flat_routes // exp_local
    home_slot = flat_routes % exp_local
    partner_host = jnp.bitwise_xor(home_host, half_axis)
    is_moved = home_slot == lookup(moving_slot, home_host, host_count)
    dest_host = jnp.where(is_moved, partner_host, home_host)
    dest_slot = jnp.where(is_moved, lookup(moving_slot, partner_host, host_count), home_slot)
    expert_hits = (
        flat_routes[:, None] == jnp.arange(expert_count, dtype=jnp.int32)[None, :]
    ).astype(jnp.int32)
    running = jnp.cumsum(expert_hits, axis=0)
    slot_rank = jnp.sum(running * expert_hits, axis=1) - 1
    flat_slot = (dest_slot * host_count + dest_host) * capacity + slot_rank
    slot_table = (
        jnp.full((total_slots,), pair_count, jnp.int32)
        .at[flat_slot]
        .set(jnp.arange(pair_count, dtype=jnp.int32))
    )
    is_live = slot_table < pair_count
    safe_pair = jnp.minimum(slot_table, pair_count - 1)
    source_row = safe_pair // top_count
    rows_send = jnp.where(is_live[:, None], tokens[source_row], 0).reshape(
        exp_local, host_count, capacity, width
    )
    cot_send = jnp.where(is_live[:, None], out_grad[source_row], 0).reshape(
        exp_local, host_count, capacity, width
    )
    gate_send = jnp.where(is_live, gates.reshape(-1)[safe_pair], 0).reshape(
        exp_local, host_count, capacity
    )
    recv_rows, recv_cot, recv_gate = (
        lax.all_to_all(rows_send, "expert", split_axis=1, concat_axis=1, tiled=True),
        lax.all_to_all(cot_send, "expert", split_axis=1, concat_axis=1, tiled=True),
        lax.all_to_all(gate_send, "expert", split_axis=1, concat_axis=1, tiled=True),
    )
    recv_rows = recv_rows.reshape(exp_local, host_count * capacity, width)
    recv_cot = recv_cot.reshape(exp_local, host_count * capacity, width)
    recv_gate = recv_gate.reshape(exp_local, host_count * capacity)
    scaled_cot = (recv_gate.astype(jnp.float32)[..., None] * recv_cot.astype(jnp.float32)).astype(
        jnp.bfloat16
    )
    expert_out, row_grad, gate_up_part, down_part = expert_block(
        recv_rows, scaled_cot, gate_up_local, down_local, hidden_width
    )
    back_out = expert_out.reshape(exp_local, host_count, capacity, width)
    back_grad = row_grad.reshape(exp_local, host_count, capacity, width)
    ret_out, ret_grad = (
        lax.all_to_all(back_out, "expert", split_axis=1, concat_axis=1, tiled=True),
        lax.all_to_all(back_grad, "expert", split_axis=1, concat_axis=1, tiled=True),
    )
    pair_out = ret_out.reshape(total_slots, width)[flat_slot].reshape(rows_local, top_count, width)
    pair_grad = ret_grad.reshape(total_slots, width)[flat_slot].reshape(
        rows_local, top_count, width
    )
    mixed = jnp.sum(
        gates.astype(jnp.float32)[..., None] * pair_out.astype(jnp.float32), axis=1
    ).astype(jnp.bfloat16)
    token_grad = jnp.sum(pair_grad.astype(jnp.float32), axis=1).astype(jnp.bfloat16)
    summed_gate_up, summed_down = (
        lax.psum_scatter(
            gate_up_part.astype(jnp.bfloat16), "dp", scatter_dimension=1, tiled=True
        ).astype(jnp.float32),
        lax.psum_scatter(
            down_part.astype(jnp.bfloat16), "dp", scatter_dimension=2, tiled=True
        ).astype(jnp.float32),
    )
    gate_up_grad = summed_gate_up.astype(jnp.bfloat16)
    down_grad = summed_down.astype(jnp.bfloat16)
    return (mixed, token_grad, gate_up_grad, down_grad)


def solution(mesh):
    placed = (
        P(("dp", "expert"), None),
        P(("dp", "expert"), None),
        P(("dp", "expert"), None),
        P(("dp", "expert"), None),
        P("expert", None, None),
        P("expert", None, None),
        P(),
    )
    return jax.shard_map(
        on_device,
        mesh=mesh,
        in_specs=placed,
        out_specs=(
            P(("dp", "expert"), None),
            P(("dp", "expert"), None),
            P("expert", "dp", None),
            P("expert", None, "dp"),
        ),
        check_vma=False,
    )
```

profile of v0, /device:TPU:0, one launch (start us, length us, event | category | flops | bytes accessed | tf_op | source)
XLA Modules:
  0.0 685.8 jit_solution(17318135598936552021)
XLA Ops:
  7.2 10.5 %copy.128 = bf16[2,2048,1408]{2,1,0:T(8,128)(2,1)} copy(bf16[2,2048,1408]{2,1,0:T(8,128)(2,1)} %param.11) | data formatting | bytes 23068672
  26.9 6.8 gather_fusion.2
  34.4 9.3 %all-to-all-start.2 = ((bf16[2,32,16]{2,0,1:T(2,128)(2,1)}), bf16[2,32,16]{2,0,1:T(2,128)(2,1)S(1)}, u32[]{:S(2)}, u32[]{:S(2)}) async-start(bf16[2,32,16]{2,0,1:T(2,128)(2,1)} %copy.106), calls=%async_computation.2 | async-start | bytes 32768 | tf_op jit(solution)/shard_map/all_to_all | solution.py:100
  43.8 6.0 gather_fusion.3
  49.8 6.1 gather_fusion
  55.9 6.0 copy_select_fusion
  61.9 8.4 %all-to-all-start = ((bf16[2,32,16,2048]{3,2,0,1:T(8,128)(2,1)}), bf16[2,32,16,2048]{3,2,0,1:T(8,128)(2,1)}, u32[]{:S(2)}, u32[]{:S(2)}) async-start(bf16[2,32,16,2048]{3,2,0,1:T(8,128)(2,1)} %get-tuple-element.12), calls=%async_computation | async-start | bytes 8388608 | tf_op jit(solution)/shard_map/all_to_all | solution.py:98
  72.9 5.6 dynamic-slice_bitcast_fusion
  81.7 164.1 %all-to-all-done = bf16[2,32,16,2048]{3,2,0,1:T(8,128)(2,1)} async-done(((bf16[2,32,16,2048]{3,2,0,1:T(8,128)(2,1)}), bf16[2,32,16,2048]{3,2,0,1:T(8,128)(2,1)}, u32[]{:S(2)}, u32[]{:S(2)}) %all-to-all-start) | async-done | bytes 4194336 | tf_op jit(solution)/shard_map/all_to_all | solution.py:98
  245.8 7.1 %all-to-all-start.3 = ((bf16[2,32,16,2048]{3,2,0,1:T(8,128)(2,1)}), bf16[2,32,16,2048]{3,2,0,1:T(8,128)(2,1)}, u32[]{:S(2)}, u32[]{:S(2)}) async-start(bf16[2,32,16,2048]{3,2,0,1:T(8,128)(2,1)} %get-tuple-element.11), calls=%async_computation.3 | async-start | bytes 8388608 | tf_op jit(solution)/shard_map/all_to_all | solution.py:99
  260.7 102.6 %collective-permute-done.1 = bf16[704,2048]{1,0:T(8,128)(2,1)S(1)} collective-permute-done((bf16[704,2048]{1,0:T(8,128)(2,1)}, bf16[704,2048]{1,0:T(8,128)(2,1)S(1)}, u32[]{:S(2)}, u32[]{:S(2)}) %collective-permute-start.1) | collective-permute-done | bytes 2883616 | tf_op jit(solution)/shard_map/ppermute | solution.py:10
  365.0 4.8 copy.100
  375.4 5.7 bitcast_dynamic-update-slice_fusion
  381.1 15.9 %fusion.17 = f32[2,512,1408]{1,2,0:T(8,128)} fusion(bf16[2,512,2048]{2,1,0:T(8,128)(2,1)} %bitcast.51, bf16[2,2048,1408]{2,1,0:T(8,128)(2,1)} %bitcast_dynamic-update-slice_fusion), kind=kOutput, calls=%fused_computation.72 | convolution fusion | flops 5905580032 | bytes 21495808 | tf_op jit(solution)/shard_map/snd,sdf->snf/dot_general | solution.py:19
  397.0 8.9 %multiply_convert_fusion.1 = (bf16[2,512,704]{1,2,0:T(8,128)(2,1)}, bf16[2,512,704]{1,2,0:T(8,128)(2,1)}, bf16[2,512,704]{1,2,0:T(8,128)(2,1)S(1)}) fusion(f32[2,512,1408]{1,2,0:T(8,128)} %fusion.17, bf16[2,512,2048]{2,1,0:T(8,128)(2,1)} %fusion, bf16[2,704,2048]{2,1,0:T(8,128)(2,1)S(1)} %bitcast.50), kind=kOutput, calls=%fused_computation.20 | convolution fusion | flops 2963603456 | bytes 20054016 | tf_op jit(solution)/shard_map/snd,sfd->snf/dot_general | solution.py:30
  405.9 5.0 convolution_convert_fusion.1
  411.1 12.7 %convolution_convert_fusion = bf16[2,2048,1408]{2,1,0:T(8,128)(2,1)} fusion(bf16[2,512,2048]{2,1,0:T(8,128)(2,1)} %bitcast.52, bf16[2,512,704]{1,2,0:T(8,128)(2,1)} %get-tuple-element.9, bf16[2,512,704]{1,2,0:T(8,128)(2,1)} %get-tuple-element.8), kind=kOutput, calls=%fused_computation.6 | convolution fusion | flops 5917114368 | bytes 18612224 | tf_op jit(solution)/shard_map/snd,snf->sdf/dot_general | solution.py:40
  423.8 7.3 %convolution_convert_fusion.3 = bf16[2,512,2048]{2,1,0:T(8,128)(2,1)S(1)} fusion(bf16[2,512,704]{1,2,0:T(8,128)(2,1)S(1)} %get-tuple-element.10, bf16[2,704,2048]{2,1,0:T(8,128)(2,1)} %bitcast_dynamic-update-slice_fusion.1), kind=kOutput, calls=%fused_computation.16 | convolution fusion | flops 2954887168 | bytes 11403264 | tf_op jit(solution)/shard_map/snf,sfd->snd/dot_general | solution.py:27
  433.6 12.5 %all-to-all-start.1 = ((bf16[2,32,16,2048]{3,2,0,1:T(8,128)(2,1)}), bf16[2,32,16,2048]{3,2,0,1:T(8,128)(2,1)}, u32[]{:S(2)}, u32[]{:S(2)}) async-start(bf16[2,32,16,2048]{3,2,0,1:T(8,128)(2,1)} %copy.103), calls=%async_computation.1 | async-start | bytes 8388608 | tf_op jit(solution)/shard_map/all_to_all | solution.py:114
  446.1 10.3 %convolution_convert_fusion.2 = bf16[2,512,2048]{2,1,0:T(8,128)(2,1)S(1)} fusion(bf16[2,2048,1408]{2,1,0:T(8,128)(2,1)} %bitcast_dynamic-update-slice_fusion, bf16[2,512,704]{1,2,0:T(8,128)(2,1)S(1)} %copy-done.9, bf16[2,512,704]{1,2,0:T(8,128)(2,1)S(1)} %copy-done.8), kind=kOutput, calls=%fused_computation.15 | convolution fusion | flops 5913444352 | bytes 18612224 | tf_op jit(solution)/shard_map/snf,sdf->snd/dot_general | solution.py:36
  458.8 48.4 %all-to-all-done.1 = bf16[2,32,16,2048]{3,2,0,1:T(8,128)(2,1)} async-done(((bf16[2,32,16,2048]{3,2,0,1:T(8,128)(2,1)}), bf16[2,32,16,2048]{3,2,0,1:T(8,128)(2,1)}, u32[]{:S(2)}, u32[]{:S(2)}) %all-to-all-start.1) | async-done | bytes 4194336 | tf_op jit(solution)/shard_map/all_to_all | solution.py:114
  507.2 9.3 %all-to-all-start.4 = ((bf16[2,32,16,2048]{3,2,0,1:T(8,128)(2,1)}), bf16[2,32,16,2048]{3,2,0,1:T(8,128)(2,1)}, u32[]{:S(2)}, u32[]{:S(2)}) async-start(bf16[2,32,16,2048]{3,2,0,1:T(8,128)(2,1)} %copy.112), calls=%async_computation.4 | async-start | bytes 8388608 | tf_op jit(solution)/shard_map/all_to_all | solution.py:115
  516.6 4.8 copy.104
  521.4 9.8 %gather_fusion.1 = bf16[768,2048]{1,0:T(8,128)(2,1)} fusion(bf16[1024,2048]{1,0:T(8,128)(2,1)} %bitcast.46, s32[1024]{0:T(1024)S(1)} %pad_clamp_fusion), kind=kCustom, calls=%fused_computation.1 | custom fusion | bytes 6294528 | tf_op jit(solution)/shard_map/gather | solution.py:117
  531.3 6.6 reshape.258
  537.8 35.5 %all-to-all-done.4 = bf16[2,32,16,2048]{3,2,0,1:T(8,128)(2,1)} async-done(((bf16[2,32,16,2048]{3,2,0,1:T(8,128)(2,1)}), bf16[2,32,16,2048]{3,2,0,1:T(8,128)(2,1)}, u32[]{:S(2)}, u32[]{:S(2)}) %all-to-all-start.4) | async-done | bytes 4194336 | tf_op jit(solution)/shard_map/all_to_all | solution.py:115
  573.3 4.8 copy.113
  578.1 9.8 %gather_fusion.4 = bf16[768,2048]{1,0:T(8,128)(2,1)} fusion(bf16[1024,2048]{1,0:T(8,128)(2,1)} %bitcast.45, s32[1024]{0:T(1024)S(1)} %pad_clamp_fusion), kind=kCustom, calls=%fused_computation.4 | custom fusion | bytes 6294528 | tf_op jit(solution)/shard_map/gather | solution.py:118
  587.9 7.0 %reshape.257 = bf16[128,6,2048]{2,1,0:T(8,128)(2,1)} reshape(bf16[768,2048]{1,0:T(8,128)(2,1)} %gather_fusion.4) | data formatting | bytes 6291456 | tf_op jit(solution)/shard_map/reshape | solution.py:118
  594.9 6.9 reduce_sum.58
  601.8 7.4 %multiply_reduce_fusion = bf16[128,2048]{1,0:T(8,128)(2,1)} fusion(f32[128,6,2048]{2,1,0:T(8,128)} %reshape.258, f32[128,6]{1,0:T(8,128)S(1)} %copy.93), kind=kLoop, calls=%fused_computation.9 | loop fusion | flops 2883584 | bytes 6818816 | tf_op jit(solution)/shard_map/reduce_sum | solution.py:121
  609.2 69.5 %reduce-scatter.3.cloned.1.call-done = bf16[2,512,1408]{2,1,0:T(8,128)(2,1)} async-done(((bf16[2,2048,1408]{2,1,0:T(8,128)(2,1)}), bf16[2,512,1408]{2,1,0:T(8,128)(2,1)}) %reduce-scatter.3.cloned.1.call-update) | async-done | bytes 2883600 | tf_op jit(solution)/shard_map/reduce_scatter | solution.py:126
  (71 shorter events, 34.0 us)
Async XLA Ops:
  7.2 36.6 %copy-start = (bf16[128,2048]{1,0:T(8,128)(2,1)S(1)}, bf16[128,2048]{1,0:T(8,128)(2,1)}, u32[]{:S(2)}) copy-start(bf16[128,2048]{1,0:T(8,128)(2,1)} %param.10) | copy-start | bytes 1572868
  7.2 10.5 %copy-start.3 = (bf16[2,704,2048]{2,1,0:T(8,128)(2,1)S(1)}, bf16[2,704,2048]{2,1,0:T(8,128)(2,1)}, u32[]{:S(2)}) copy-start(bf16[2,704,2048]{2,1,0:T(8,128)(2,1)} %param.12) | copy-start | bytes 17301508
  17.7 2.5 copy-start.6
  17.7 5.3 copy-start.7
  17.7 8.9 %copy-start.5 = (bf16[128,6]{0,1:T(8,128)(2,1)S(1)}, bf16[128,6]{0,1:T(8,128)(2,1)}, u32[]{:S(2)}) copy-start(bf16[128,6]{0,1:T(8,128)(2,1)} %param.9) | copy-start | bytes 4612
  34.4 27.5 %all-to-all-start.2 = ((bf16[2,32,16]{2,0,1:T(2,128)(2,1)}), bf16[2,32,16]{2,0,1:T(2,128)(2,1)S(1)}, u32[]{:S(2)}, u32[]{:S(2)}) async-start(bf16[2,32,16]{2,0,1:T(2,128)(2,1)} %copy.106), calls=%async_computation.2 | async-start | bytes 32768 | tf_op jit(solution)/shard_map/all_to_all | solution.py:100
  43.8 6.0 copy-start.2
  61.9 183.9 %all-to-all-start = ((bf16[2,32,16,2048]{3,2,0,1:T(8,128)(2,1)}), bf16[2,32,16,2048]{3,2,0,1:T(8,128)(2,1)}, u32[]{:S(2)}, u32[]{:S(2)}) async-start(bf16[2,32,16,2048]{3,2,0,1:T(8,128)(2,1)} %get-tuple-element.12), calls=%async_computation | async-start | bytes 8388608 | tf_op jit(solution)/shard_map/all_to_all | solution.py:98
  78.5 296.9 %collective-permute-start = (bf16[2048,1408]{1,0:T(8,128)(2,1)}, bf16[2048,1408]{1,0:T(8,128)(2,1)}, u32[]{:S(2)}, u32[]{:S(2)}) collective-permute-start(bf16[2048,1408]{1,0:T(8,128)(2,1)} %dynamic-slice_bitcast_fusion), channel_id=1, source_target_pairs={{0,16},{1,17},{2,18},{3,19},{4,20},{5,21},{6,22},{7,23},{8,24},{9,... | collective-permute-start | bytes 17301512 | tf_op jit(solution)/shard_map/ppermute | solution.py:10
  245.8 124.1 %all-to-all-start.3 = ((bf16[2,32,16,2048]{3,2,0,1:T(8,128)(2,1)}), bf16[2,32,16,2048]{3,2,0,1:T(8,128)(2,1)}, u32[]{:S(2)}, u32[]{:S(2)}) async-start(bf16[2,32,16,2048]{3,2,0,1:T(8,128)(2,1)} %get-tuple-element.11), calls=%async_computation.3 | async-start | bytes 8388608 | tf_op jit(solution)/shard_map/all_to_all | solution.py:99
  252.9 356.3 %reduce-scatter.5.cloned.1.call-start = ((), (), s32[]{:S(2)}) async-start(), calls=%async_computation.8 | async-start | bytes 7208960 | tf_op jit(solution)/shard_map/reduce_scatter | solution.py:129
  256.7 106.6 %collective-permute-start.1 = (bf16[704,2048]{1,0:T(8,128)(2,1)}, bf16[704,2048]{1,0:T(8,128)(2,1)S(1)}, u32[]{:S(2)}, u32[]{:S(2)}) collective-permute-start(bf16[704,2048]{1,0:T(8,128)(2,1)} %dynamic-slice_bitcast_fusion.1), channel_id=1, source_target_pairs={{0,16},{1,17},{2,18},{3,19},{4,20},{5,21},{6,22},{7,23},{8,24},{9,... | collective-permute-start | bytes 8650760 | tf_op jit(solution)/shard_map/ppermute | solution.py:10
  375.4 21.6 %slice-start = ((s8[5767168]{0:T(1024)(128)(4,1)}), s8[4194304]{0:T(1024)(128)(4,1)S(1)}, s32[]{:S(2)}) async-start(s8[5767168]{0:T(1024)(128)(4,1)} %bitcast.49), calls=%async_computation.9 | async-start | bytes 8388608
  381.1 15.9 %slice-start.1 = ((s8[5767168]{0:T(1024)(128)(4,1)}), s8[1572864]{0:T(1024)(128)(4,1)S(1)}, s32[]{:S(2)}) async-start(s8[5767168]{0:T(1024)(128)(4,1)} %bitcast.49), calls=%async_computation.10 | async-start | bytes 3145728
  397.0 8.9 %copy-start.4 = (bf16[2,512,2048]{2,1,0:T(8,128)(2,1)S(1)}, bf16[2,512,2048]{2,1,0:T(8,128)(2,1)}, u32[]{:S(2)}) copy-start(bf16[2,512,2048]{2,1,0:T(8,128)(2,1)} %fusion) | copy-start | bytes 12582916
  410.9 267.8 %reduce-scatter.3.cloned.1.call-start = ((), (), s32[]{:S(2)}) async-start(), calls=%async_computation.7 | async-start | bytes 14417920 | tf_op jit(solution)/shard_map/reduce_scatter | solution.py:126
  433.6 12.5 %copy-start.8 = (bf16[2,512,704]{1,2,0:T(8,128)(2,1)S(1)}, bf16[2,512,704]{1,2,0:T(8,128)(2,1)}, u32[]{:S(2)}) copy-start(bf16[2,512,704]{1,2,0:T(8,128)(2,1)} %get-tuple-element.8) | copy-start | bytes 4325380
  433.6 12.6 %copy-start.9 = (bf16[2,512,704]{1,2,0:T(8,128)(2,1)S(1)}, bf16[2,512,704]{1,2,0:T(8,128)(2,1)}, u32[]{:S(2)}) copy-start(bf16[2,512,704]{1,2,0:T(8,128)(2,1)} %get-tuple-element.9) | copy-start | bytes 4325380
  433.6 73.6 %all-to-all-start.1 = ((bf16[2,32,16,2048]{3,2,0,1:T(8,128)(2,1)}), bf16[2,32,16,2048]{3,2,0,1:T(8,128)(2,1)}, u32[]{:S(2)}, u32[]{:S(2)}) async-start(bf16[2,32,16,2048]{3,2,0,1:T(8,128)(2,1)} %copy.103), calls=%async_computation.1 | async-start | bytes 8388608 | tf_op jit(solution)/shard_map/all_to_all | solution.py:114
  507.2 66.1 %all-to-all-start.4 = ((bf16[2,32,16,2048]{3,2,0,1:T(8,128)(2,1)}), bf16[2,32,16,2048]{3,2,0,1:T(8,128)(2,1)}, u32[]{:S(2)}, u32[]{:S(2)}) async-start(bf16[2,32,16,2048]{3,2,0,1:T(8,128)(2,1)} %copy.112), calls=%async_computation.4 | async-start | bytes 8388608 | tf_op jit(solution)/shard_map/all_to_all | solution.py:115
  594.9 83.8 %copy-start.1 = (bf16[128,2048]{1,0:T(8,128)(2,1)S(1)}, bf16[128,2048]{1,0:T(8,128)(2,1)}, u32[]{:S(2)}) copy-start(bf16[128,2048]{1,0:T(8,128)(2,1)} %param.10) | copy-start | bytes 1572868
Sparse Core Ops, SparseCore 0:
  411.0 124.2 reduce-scatter.4
  538.8 139.8 reduce-scatter.2
where the time goes:
time: 692 us; the launch traced here: 686 us
  waiting for transfers between devices  420 us (61%)
  local copies, waits for them, and re-layouts  110 us (16%)
  matrix products  60.1 us (9%)
  starting transfers between devices  53.8 us (8%)
  other arithmetic  25.3 us (4%)
  between operations  16.6 us (2%)
    all_to_all x1, waiting for transfers between devices, on_device(): lax.all_to_all(rows_send, 'expert', split_axis=1, concat_axis=1, tiled=True)  164 us
    ppermute x2, waiting for transfers between devices, from_partner(): return lax.ppermute(value, axis, pairs)  103 us
    reduce_scatter x1, waiting for transfers between devices, on_device(): lax.psum_scatter(gate_up_part.astype(jnp.bfloat16), 'dp', scatter_dimensi...  69.5 us
    all_to_all x1, waiting for transfers between devices, on_device(): lax.all_to_all(back_out, 'expert', split_axis=1, concat_axis=1, tiled=True)  48.4 us
    all_to_all x1, waiting for transfers between devices, on_device(): lax.all_to_all(back_grad, 'expert', split_axis=1, concat_axis=1, tiled=True)  35.5 us
    dot_general x1, matrix products, expert_block(): jnp.einsum('snd,sdf->snf', recv_rows, gate_up_local, preferred_element_ty...  15.9 us
  transfers between devices with their start and end apart: 9, of which 5 were waited for; matrix products, arithmetic and copies ran while one was open for 19% of the time, Pallas kernels for 0%

commit v1 on v0

v1 whole, which is shorter than its diff:
```python
import jax
import jax.numpy as jnp
from jax import lax
from jax.experimental import pallas as pl
from jax.experimental.pallas import tpu as pltpu
from jax.sharding import PartitionSpec as P

MESH = pl.DeviceIdType.MESH
BF, F32 = jnp.bfloat16, jnp.float32

ROWS, WIDTH, HID, TOP, CAP = 128, 2048, 704, 6, 16
FULL = 2 * HID
QUARTER = WIDTH // 4

OUTBOUND = ((0, 1, 2, 0, 640), (1, 2, 0, 640, 640), (2, 0, 1, 1280, 768))
INBOUND = ((0, 1, 2, 0, 640), (1, 2, 0, 640, 640), (2, 0, 1, 1280, 768))


def device_at(x, y, z, core):
    return ((y // 2) * 2 + core, x * 8 + (y % 2) * 4 + z)


def dot(a, b, contract):
    return lax.dot_general(a, b, ((contract[:1], contract[1:]), ((), ())), preferred_element_type=F32)


def kernel(
    moving, tokens, routes, gates, out_grad, gate_up, down,
    mixed, token_grad, stay_gu, stay_dn, got_gu, got_dn, fwd1, fwd2, bck1, bck2,
    near1, near2, pick1, pick2, slot1, slot2, w_gu, w_dn, pre, hid, pre_grad,
    back1, back2, part1, part2, core_gu, core_dn, lane_gu, lane_dn, info, onehot, gated,
    sends, recvs, info_send, info_recv, local_sem, w_sem, grad_send, grad_recv, out_sem,
):
    dp, ex = lax.axis_index("dp"), lax.axis_index("expert")
    y_hi, core = dp // 2, dp % 2
    me = (ex // 8, y_hi * 2 + (ex // 4) % 2, ex % 4)

    def along(axis, step):
        place = list(me)
        place[axis] = (place[axis] + step) % 4
        return device_at(*place, core)

    other_core = device_at(*me, 1 - core)

    barrier = pltpu.get_barrier_semaphore()
    for axis in range(3):
        for step in (1, 2, 3):
            pl.semaphore_signal(barrier, inc=1, device_id=along(axis, step), device_id_type=MESH)
    pl.semaphore_signal(barrier, inc=1, device_id=other_core, device_id_type=MESH)

    load_gu = pltpu.make_async_copy(gate_up.at[y_hi], w_gu, w_sem.at[0])
    load_dn = pltpu.make_async_copy(down.at[y_hi], w_dn, w_sem.at[1])
    load_gu.start()
    load_dn.start()
    pl.semaphore_wait(barrier, 10)

    def send(src, dst, send_sem, recv_sem, device):
        copy = pltpu.make_async_remote_copy(
            src_ref=src, dst_ref=dst, send_sem=send_sem, recv_sem=recv_sem,
            device_id=device, device_id_type=MESH,
        )
        copy.start()
        return copy

    def keep(src, dst, sem):
        copy = pltpu.make_async_copy(src, dst, sem)
        copy.start()
        return copy

    def wait_all(copies):
        for copy in copies:
            copy.wait()

    def fixed(axis, index, ref, columns):
        spot = [slice(None)] * 3
        spot[axis] = index
        return ref.at[(*spot, slice(None), columns)]

    def gather_axis(stage, source, near):
        started = []
        for q, (a, _, _, first, count) in enumerate(OUTBOUND):
            columns = pl.ds(first, count)
            started.append([
                send(source.at[:, columns], near.at[step, :, columns],
                     sends.at[stage, q, step - 1], recvs.at[stage, q, step - 1], along(a, step))
                for step in (1, 3, 2)
            ])
        return started

    gather1 = gather_axis(0, tokens, near1)

    lane = lax.broadcasted_iota(jnp.int32, (ROWS, 128), 1)
    name = lane % 64
    hits = jnp.zeros((ROWS, 128), F32)
    weight = jnp.zeros((ROWS, 128), F32)
    all_routes, all_gates = routes[...], gates[...].astype(F32)
    for k in range(TOP):
        same = all_routes[:, k : k + 1] == name
        hits = hits + jnp.where(same, 1.0, 0.0)
        weight = weight + jnp.where(same, all_gates[:, k : k + 1], 0.0)
    below = lax.broadcasted_iota(jnp.int32, (ROWS, ROWS), 1) < lax.broadcasted_iota(
        jnp.int32, (ROWS, ROWS), 0
    )
    rank = dot(jnp.where(below, 1.0, 0.0).astype(BF), hits.astype(BF), (1, 0))
    own_info = jnp.where(lane < 64, jnp.where(hits > 0.5, rank, 99.0), weight).astype(BF)
    for axis in range(3):
        info[axis, 0] = own_info
    info_copies = [
        [
            send(info.at[axis, 0], info.at[axis, step],
                 info_send.at[axis, step - 1], info_recv.at[axis, step - 1], along(axis, step))
            for step in (1, 3, 2)
        ]
        for axis in range(3)
    ]
    gather2 = gather_axis(1, out_grad, near2)
    near1[0] = tokens[...]
    near2[0] = out_grad[...]

    def pick_masks(axis, b, c):
        row = lax.broadcasted_iota(jnp.int32, (128, 256), 0)
        column = lax.broadcasted_iota(jnp.int32, (128, 256), 1)
        place = [None, None, None]
        place[axis], place[b], place[c] = me[axis], column // 64, (column // 16) % 4
        expert = 2 * (place[0] * 8 + (place[1] % 2) * 4 + place[2]) + place[1] // 2
        choose_rank = jnp.where(row == expert, 1.0, 0.0).astype(BF)
        choose_gate = jnp.where(row == expert + 64, 1.0, 0.0).astype(BF)
        number = (lax.broadcasted_iota(jnp.int32, (ROWS, 256), 1) % 16).astype(F32)

        def one(step, _):
            ranks = dot(info[axis, step], choose_rank, (1, 0))
            scale = dot(info[axis, step], choose_gate, (1, 0))
            live = ranks == number
            onehot[axis, step] = jnp.where(live, 1.0, 0.0).astype(BF)
            gated[axis, step] = jnp.where(live, scale, 0.0).astype(BF)
            return 0

        lax.fori_loop(0, 4, one, 0)

    def pick(chunk, near, masks, picked):
        a, _, _, first, count = chunk

        def one(step, _):
            rows = dot(masks[a, step], near[step, :, first : first + count], (0, 0))
            source = (me[a] - step + 4) % 4
            picked[:, :, source, :, first : first + count] = rows.astype(BF).reshape(4, 4, 16, count)
            return 0

        lax.fori_loop(0, 4, one, 0)

    def second_axis(stage, q, picked, onward):
        a, b, _, first, count = OUTBOUND[q]
        columns = pl.ds(first, count)
        landing = (
            onward.at[:, :, me[b], :, columns] if a < b else onward.at[:, me[b], :, :, columns]
        )
        copies = [
            send(picked.at[(me[b] + step) % 4, :, :, :, columns], landing,
                 sends.at[stage, q, step - 1], recvs.at[stage, q, step - 1], along(b, step))
            for step in (1, 3, 2)
        ]
        copies.append(keep(picked.at[me[b], :, :, :, columns], landing, local_sem.at[stage, q]))
        return copies

    def third_axis(stage, q, onward, slots):
        _, _, c, first, count = OUTBOUND[q]
        columns = pl.ds(first, count)
        landing = fixed(c, me[c], slots, columns)
        copies = [
            send(onward.at[(me[c] + step) % 4, :, :, :, columns], landing,
                 sends.at[stage, q, step - 1], recvs.at[stage, q, step - 1], along(c, step))
            for step in (1, 3, 2)
        ]
        copies.append(keep(onward.at[me[c], :, :, :, columns], landing, local_sem.at[stage, q]))
        return copies

    spread1, spread2, final1, final2 = [], [], [], []
    for q, chunk in enumerate(OUTBOUND):
        wait_all(info_copies[chunk[0]])
        pick_masks(chunk[0], chunk[1], chunk[2])
        wait_all(gather1[q])
        pick(chunk, near1, onehot, pick1)
        spread1.append(second_axis(2, q, pick1, fwd1))
    for q, chunk in enumerate(OUTBOUND):
        wait_all(gather2[q])
        pick(chunk, near2, gated, pick2)
        spread2.append(second_axis(3, q, pick2, fwd2))
    for q in range(len(OUTBOUND)):
        wait_all(spread1[q])
        final1.append(third_axis(4, q, fwd1, slot1))
    for q in range(len(OUTBOUND)):
        wait_all(spread2[q])
        final2.append(third_axis(5, q, fwd2, slot2))

    load_gu.wait()
    load_dn.wait()
    for copies in final1:
        wait_all(copies)

    def forward(m, _):
        rows = slot1[m].reshape(256, WIDTH)
        projected = dot(rows, w_gu[...], (1, 0))
        here = pl.ds(pl.multiple_of(m * 256, 256), 256)
        pre[here] = projected
        pre_gate = projected[:, :HID]
        pre_up = projected[:, HID:]
        hidden = (pre_gate * jax.nn.sigmoid(pre_gate) * pre_up).astype(BF)
        hid[here] = hidden
        pick1[m] = dot(hidden, w_dn[...], (1, 0)).astype(BF).reshape(4, 4, 16, WIDTH)
        return 0

    lax.fori_loop(0, 4, forward, 0)

    def first_back(stage, result, onward):
        started = []
        for q, (_, _, c, first, count) in enumerate(INBOUND):
            columns = pl.ds(first, count)
            landing = onward.at[me[c], :, :, :, columns]
            copies = [
                send(fixed(c, (me[c] + step) % 4, result, columns), landing,
                     sends.at[stage, q, step - 1], recvs.at[stage, q, step - 1], along(c, step))
                for step in (1, 3, 2)
            ]
            copies.append(keep(fixed(c, me[c], result, columns), landing, local_sem.at[stage, q]))
            started.append(copies)
        return started

    def second_back(stage, q, onward, back):
        a, b, _, first, count = INBOUND[q]
        columns = pl.ds(first, count)

        def to(index):
            return onward.at[:, :, index, :, columns] if a < b else onward.at[:, index, :, :, columns]

        landing = back.at[me[b], :, :, :, columns]
        copies = [
            send(to((me[b] + step) % 4), landing,
                 sends.at[stage, q, step - 1], recvs.at[stage, q, step - 1], along(b, step))
            for step in (1, 3, 2)
        ]
        copies.append(keep(to(me[b]), landing, local_sem.at[stage, q]))
        return copies

    def combine(stage, q, back, masks, near, part):
        a, _, _, first, count = INBOUND[q]

        def one(step, _):
            target = (me[a] + step) % 4
            rows = back[:, :, target, :, first : first + count].reshape(256, count)
            near[step, :, first : first + count] = dot(
                masks[a, (4 - step) % 4], rows, (1, 0)
            ).astype(BF)
            return 0

        lax.fori_loop(0, 4, one, 0)
        columns = pl.ds(first, count)
        return [
            send(near.at[step, :, columns], part.at[step - 1, :, columns],
                 sends.at[stage, q, step - 1], recvs.at[stage, q, step - 1], along(a, step))
            for step in (1, 3, 2)
        ]

    home1 = first_back(6, pick1, bck1)

    for copies in final2:
        wait_all(copies)

    def backward(m, _):
        scaled = slot2[m].reshape(256, WIDTH)
        hidden_grad = dot(scaled, w_dn[...], (1, 1))
        here = pl.ds(pl.multiple_of(m * 256, 256), 256)
        projected = pre[here]
        pre_gate = projected[:, :HID]
        pre_up = projected[:, HID:]
        sigmoid_gate = jax.nn.sigmoid(pre_gate)
        grad_gate = hidden_grad * pre_up * sigmoid_gate * (1.0 + pre_gate * (1.0 - sigmoid_gate))
        grad_up = hidden_grad * (pre_gate * sigmoid_gate)
        both = jnp.concatenate([grad_gate, grad_up], axis=1).astype(BF)
        pre_grad[here] = both
        pick2[m] = dot(both, w_gu[...], (1, 1)).astype(BF).reshape(4, 4, 16, WIDTH)
        return 0

    lax.fori_loop(0, 4, backward, 0)
    home2 = first_back(7, pick2, bck2)

    turn1, turn2 = [], []
    for q in range(len(INBOUND)):
        wait_all(home1[q])
        turn1.append(second_back(8, q, bck1, back1))

    quarters = [
        pl.multiple_of(QUARTER * (2 * hi + c), QUARTER)
        for c in (1 - core, core)
        for hi in (1 - y_hi, y_hi)
    ]

    def gradients(first, from_core):
        def one(t, _):
            here = pl.ds(pl.multiple_of(first + t * 256, 256), 256)
            there = pl.ds(pl.multiple_of(t * 256, 256), 256)
            rows = slot1[:, :, :, :, here].reshape(1024, 256)
            result = dot(rows, pre_grad[...], (0, 0))
            if from_core is not None:
                result = result + core_gu[from_core, there].astype(F32)
            w_gu[here] = result.astype(BF)
            scaled = slot2[:, :, :, :, here].reshape(1024, 256)
            result = dot(hid[...], scaled, (0, 0))
            if from_core is not None:
                result = result + core_dn[from_core, :, there].astype(F32)
            w_dn[:, here] = result.astype(BF)
            return 0

        lax.fori_loop(0, 2, one, 0)

    to_core = []
    for j in range(2):
        gradients(quarters[j], None)
        part_of = pl.ds(quarters[j], QUARTER)
        to_core.append([
            send(w_gu.at[part_of], core_gu.at[j], grad_send.at[2 * j], grad_recv.at[2 * j], other_core),
            send(w_dn.at[:, part_of], core_dn.at[j], grad_send.at[2 * j + 1],
                 grad_recv.at[2 * j + 1], other_core),
        ])
    for q in range(len(INBOUND)):
        wait_all(home2[q])
        turn2.append(second_back(9, q, bck2, back2))

    wait_all(to_core[0])
    gradients(quarters[2], 0)
    across = []
    for p in range(2):
        across.append(send(
            w_gu.at[pl.ds(pl.multiple_of(quarters[2] + p * 256, 256), 256)],
            lane_gu.at[pl.ds(p * 256, 256)],
            grad_send.at[4 + p], grad_recv.at[4 + p], along(1, 2),
        ))
    across.append(send(
        w_dn.at[:, pl.ds(quarters[2], QUARTER)], lane_dn, grad_send.at[6], grad_recv.at[6], along(1, 2),
    ))
    wait_all(to_core[1])
    gradients(quarters[3], 1)

    last1, last2 = [], []
    for q in range(len(INBOUND)):
        wait_all(turn1[q])
        last1.append(combine(10, q, back1, gated, near1, part1))

    moves_own = moving[ex] == y_hi
    relocated, stayed = [], []
    for p in range(2):
        across[p].wait()
        mine = w_gu[pl.ds(pl.multiple_of(quarters[3] + p * 256, 256), 256)]
        theirs = lane_gu[pl.ds(p * 256, 256)]
        out_rows = pl.ds(pl.multiple_of(quarters[0] + p * 256, 256), 256)
        stay_rows = pl.ds(pl.multiple_of(quarters[1] + p * 256, 256), 256)
        w_gu[out_rows] = jnp.where(moves_own, mine, theirs)
        w_gu[stay_rows] = jnp.where(moves_own, theirs, mine)
        relocated.append(send(
            w_gu.at[out_rows], got_gu.at[pl.ds(p * 256, 256)],
            grad_send.at[7 + p], grad_recv.at[7 + p], along(0, 2),
        ))
        stayed.append(keep(w_gu.at[stay_rows], stay_gu.at[pl.ds(p * 256, 256)], out_sem.at[p]))
    across[2].wait()
    mine = w_dn[:, pl.ds(quarters[3], QUARTER)]
    theirs = lane_dn[...]
    w_dn[:, pl.ds(quarters[0], QUARTER)] = jnp.where(moves_own, mine, theirs)
    w_dn[:, pl.ds(quarters[1], QUARTER)] = jnp.where(moves_own, theirs, mine)
    relocated.append(send(
        w_dn.at[:, pl.ds(quarters[0], QUARTER)], got_dn, grad_send.at[9], grad_recv.at[9], along(0, 2),
    ))
    stayed.append(keep(w_dn.at[:, pl.ds(quarters[1], QUARTER)], stay_dn, out_sem.at[2]))

    for q in range(len(INBOUND)):
        wait_all(turn2[q])
        last2.append(combine(11, q, back2, onehot, near2, part2))

    def total(copies, near, part, result):
        for q, (_, _, _, first, count) in enumerate(INBOUND):
            wait_all(copies[q])
            span = slice(first, first + count)
            summed = near[0, :, span].astype(F32)
            for step in range(3):
                summed = summed + part[step, :, span].astype(F32)
            result[:, span] = summed.astype(BF)

    total(last1, near1, part1, mixed)
    total(last2, near2, part2, token_grad)
    wait_all(stayed)
    wait_all(relocated)


def on_device(tokens, routes, gates, out_grad, expert_gate_up, expert_down, moving_slot):
    vmem, anywhere = pl.BlockSpec(memory_space=pltpu.VMEM), pl.BlockSpec(memory_space=pl.ANY)
    slots = (4, 4, 4, CAP, WIDTH)
    sds = jax.ShapeDtypeStruct
    dma = pltpu.SemaphoreType.DMA
    results = pl.pallas_call(
        kernel,
        out_shape=(
            sds((ROWS, WIDTH), BF), sds((ROWS, WIDTH), BF),
            sds((QUARTER, FULL), BF), sds((HID, QUARTER), BF),
            sds((QUARTER, FULL), BF), sds((HID, QUARTER), BF),
            sds(slots, BF), sds(slots, BF), sds(slots, BF), sds(slots, BF),
        ),
        in_specs=[pl.BlockSpec(memory_space=pltpu.SMEM), vmem, vmem, vmem, vmem, anywhere, anywhere],
        out_specs=(vmem, vmem) + (anywhere,) * 8,
        scratch_shapes=[
            pltpu.VMEM((4, ROWS, WIDTH), BF), pltpu.VMEM((4, ROWS, WIDTH), BF),
            pltpu.VMEM(slots, BF), pltpu.VMEM(slots, BF),
            pltpu.VMEM(slots, BF), pltpu.VMEM(slots, BF),
            pltpu.VMEM((WIDTH, FULL), BF), pltpu.VMEM((HID, WIDTH), BF),
            pltpu.VMEM((1024, FULL), F32), pltpu.VMEM((1024, HID), BF), pltpu.VMEM((1024, FULL), BF),
            pltpu.VMEM(slots, BF), pltpu.VMEM(slots, BF),
            pltpu.VMEM((3, ROWS, WIDTH), BF), pltpu.VMEM((3, ROWS, WIDTH), BF),
            pltpu.VMEM((2, QUARTER, FULL), BF), pltpu.VMEM((2, HID, QUARTER), BF),
            pltpu.VMEM((QUARTER, FULL), BF), pltpu.VMEM((HID, QUARTER), BF),
            pltpu.VMEM((3, 4, ROWS, 128), BF),
            pltpu.VMEM((3, 4, ROWS, 256), BF), pltpu.VMEM((3, 4, ROWS, 256), BF),
            dma((12, 3, 3)), dma((12, 3, 3)), dma((3, 3)), dma((3, 3)), dma((12, 3)), dma((2,)),
            dma((10,)), dma((10,)), dma((3,)),
        ],
        compiler_params=pltpu.CompilerParams(
            collective_id=0, has_side_effects=True, vmem_limit_bytes=64 * 2**20 - 2**16
        ),
        cost_estimate=pl.CostEstimate(flops=27 * 10**9, bytes_accessed=40 * 10**6, transcendentals=10**6),
    )(moving_slot, tokens, routes, gates, out_grad, expert_gate_up, expert_down)
    mixed, token_grad, stay_gu, stay_dn, got_gu, got_dn = results[:6]
    moved = jnp.arange(2, dtype=jnp.int32)[:, None, None] == moving_slot[lax.axis_index("expert")]
    gate_up_grad = jnp.where(moved, got_gu[None], stay_gu[None])
    down_grad = jnp.where(moved, got_dn[None], stay_dn[None])
    return mixed, token_grad, gate_up_grad, down_grad


def solution(mesh):
    rows, whole = P(("dp", "expert"), None), P("expert", None, None)
    return jax.shard_map(
        on_device,
        mesh=mesh,
        in_specs=(rows, rows, rows, rows, whole, whole, P()),
        out_specs=(rows, rows, P("expert", "dp", None), P("expert", None, "dp")),
        check_vma=False,
    )
```

time: 692 us -> 235 us (0.34)
  waiting for transfers between devices: 420 us -> 0 us
  Pallas kernels: 0 us -> 222 us
  local copies, waits for them, and re-layouts: 110 us -> 5.67 us
  matrix products: 60.1 us -> 0 us
  starting transfers between devices: 53.8 us -> 0 us
  other arithmetic: 25.3 us -> 5.81 us
  between operations: 16.6 us -> 0.67 us
    all_to_all x5 -> x0, waiting for transfers between devices: 248 us -> none  [the longest x1 164 us: on_device(): lax.all_to_all(rows_send, 'expert', split_axis=1, concat_axis=1, tiled=True)]
    pallas_call x0 -> x1, Pallas kernels: none -> 222 us  [on_device(): pl.pallas_call(kernel, out_shape=(sds((ROWS, WIDTH), BF), sds((ROWS, WIDT...]
    ppermute x2 -> x0, waiting for transfers between devices: 103 us -> none  [from_partner(): return lax.ppermute(value, axis, pairs)]
    reduce_scatter x2 -> x0, waiting for transfers between devices: 69.5 us -> none  [the longest x1 69.5 us: on_device(): lax.psum_scatter(gate_up_part.astype(jnp.bfloat16), 'dp', scatter_dimensi...]
    dot_general x6 -> x0, matrix products: 60.1 us -> none  [the longest x1 15.9 us: expert_block(): jnp.einsum('snd,sdf->snf', recv_rows, gate_up_local, preferred_element_ty...]
    all_to_all x5 -> x0, starting transfers between devices: 46.6 us -> none  [the longest x1 12.5 us: on_device(): lax.all_to_all(back_out, 'expert', split_axis=1, concat_axis=1, tiled=True)]
    gather x5 -> x0, local copies, waits for them, and re-layouts: 38.5 us -> none  [the longest x1 9.84 us: on_device(): ret_out.reshape(total_slots, width)[flat_slot]]
    all_to_all x5 -> x0, local copies, waits for them, and re-layouts: 17.2 us -> none  [the longest x1 4.85 us: on_device(): lax.all_to_all(rows_send, 'expert', split_axis=1, concat_axis=1, tiled=True)]
  transfers between devices with their start and end apart: 9 -> 0, of which waited for: 5 -> 0; matrix products, arithmetic and copies ran while one was open for 19% -> 0% of each run, Pallas kernels for 0% -> 0%
where the time goes in v1:
time: 235 us; the launch traced here: 234 us
  Pallas kernels  222 us (94%)
  other arithmetic  5.81 us (2%)
  local copies, waits for them, and re-layouts  5.67 us (2%)
    pallas_call x1, Pallas kernels, on_device(): pl.pallas_call(kernel, out_shape=(sds((ROWS, WIDTH), BF), sds((ROWS, WIDT...  222 us

profile of v1, /device:TPU:0, one launch (start us, length us, event | category | flops | bytes accessed | tf_op | source)
XLA Modules:
  0.0 234.3 jit_solution(14193008754478217079)
XLA Ops:
  0.6 1.4 copy.11.routes
  2.1 1.4 copy.12.gates
  3.5 222.2 %shard_map.102 = (bf16[128,2048]{1,0:T(8,128)(2,1)}, bf16[128,2048]{1,0:T(8,128)(2,1)}, bf16[512,1408]{1,0:T(8,128)(2,1)}, bf16[704,512]{1,0:T(8,128)(2,1)}, bf1...) custom-call(s32[32]{0:T(128)} %moving.1, ...), custom_call_target="tpu_custom_call" | custom-call | flops 27000000512 | bytes 40000000 | tf_op jit(solution)/shard_map/pallas_call | solution.py:397
  225.6 1.2 dynamic_slice.3
  226.9 0.6 iota_compare_fusion
  227.5 0.0 copy-start
  227.6 0.0 copy-start.1
  227.6 3.9 %broadcast_select_fusion = bf16[2,512,1408]{2,1,0:T(8,128)(2,1)} fusion(pred[2]{0:T(512)(128)(4,1)S(1)} %iota_compare_fusion, bf16[512,1408]{1,0:T(8,128)(2,1)} %get-tuple-element.13, bf16[512,1408]{1,0:T(8,128)(2,1)} %get-tuple-element.12), kind=kLoop, calls=%fused_computation | loop fusion | flops 1441792 | bytes 5767170 | tf_op jit(solution)/shard_map/jit(_where)/select_n | solution.py:429
  231.4 0.0 copy-start.3
  231.4 0.0 copy-start.2
  231.4 0.0 copy-done
  231.4 0.0 copy-done.1
  231.4 1.3 broadcast_select_fusion.1
  232.7 0.0 copy-done.3
  232.7 0.8 copy.15
  233.5 0.0 copy-done.2
  233.5 0.8 copy.16
Async XLA Ops:
  227.5 3.9 %copy-start = (bf16[704,512]{1,0:T(8,128)(2,1)S(1)}, bf16[704,512]{1,0:T(8,128)(2,1)}, u32[]{:S(2)}) copy-start(bf16[704,512]{1,0:T(8,128)(2,1)} %get-tuple-element.15) | copy-start | bytes 2162692
  227.6 3.9 %copy-start.1 = (bf16[704,512]{1,0:T(8,128)(2,1)S(1)}, bf16[704,512]{1,0:T(8,128)(2,1)}, u32[]{:S(2)}) copy-start(bf16[704,512]{1,0:T(8,128)(2,1)} %get-tuple-element.14) | copy-start | bytes 2162692
  231.4 1.3 copy-start.3
  231.4 2.1 copy-start.2

commit v2 on v1

v2 whole, which is shorter than its diff:
```python
import jax
import jax.numpy as jnp
from jax import lax
from jax.experimental import pallas as pl
from jax.experimental.pallas import tpu as pltpu
from jax.sharding import PartitionSpec as P

MESH = pl.DeviceIdType.MESH
BF, F32 = jnp.bfloat16, jnp.float32

ROWS, WIDTH, HID, TOP, CAP = 128, 2048, 704, 6, 16
FULL = 2 * HID
QUARTER = WIDTH // 4

OUTBOUND = (
    ((0, 1, 2, 0, 640), (1, 2, 0, 640, 640), (2, 0, 1, 1280, 768)),
    ((0, 1, 2, 0, 768), (1, 2, 0, 768, 640), (2, 0, 1, 1408, 640)),
)
INBOUND = ((0, 1, 2, 0, 768), (1, 2, 0, 768, 768), (2, 0, 1, 1536, 512))

SCHEDULE = (
    "rows_home", "turn1", "to_core", "to_core", "kept0", "across", "across", "across", "kept1",
    "turn2", "finish1", "relocate", "across", "relocate", "across", "relocate", "across",
    "finish2", "relocate", "relocate", "relocate",
)
MASKS = len({chunk[:3] for chunk in OUTBOUND[0] + OUTBOUND[1] + INBOUND})


def device_at(x, y, z, core):
    return ((y // 2) * 2 + core, x * 8 + (y % 2) * 4 + z)


def dot(a, b, contract):
    return lax.dot_general(a, b, ((contract[:1], contract[1:]), ((), ())), preferred_element_type=F32)


def kernel(
    moving, tokens, routes, gates, out_grad, gate_up, down,
    mixed, token_grad, stay_gu, stay_dn, got_gu, got_dn, fwd1, fwd2, bck1, bck2,
    near1, near2, pick1, pick2, slot1, slot2, w_gu, w_dn, hid, pre_grad,
    back1, back2, part1, part2, core_gu, core_dn, lane_gu, lane_dn, g_gu, info, gated,
    sends, recvs, info_send, info_recv, local_sem, w_sem, grad_send, grad_recv, out_sem,
):
    dp, ex = lax.axis_index("dp"), lax.axis_index("expert")
    y_hi, core = dp // 2, dp % 2
    me = (ex // 8, y_hi * 2 + (ex // 4) % 2, ex % 4)

    def along(axis, step):
        place = list(me)
        place[axis] = (place[axis] + step) % 4
        return device_at(*place, core)

    other_core = device_at(*me, 1 - core)

    barrier = pltpu.get_barrier_semaphore()
    for axis in range(3):
        for step in (1, 2, 3):
            pl.semaphore_signal(barrier, inc=1, device_id=along(axis, step), device_id_type=MESH)
    pl.semaphore_signal(barrier, inc=1, device_id=other_core, device_id_type=MESH)

    load_gu = pltpu.make_async_copy(gate_up.at[y_hi], w_gu, w_sem.at[0])
    load_dn = pltpu.make_async_copy(down.at[y_hi], w_dn, w_sem.at[1])
    load_gu.start()
    load_dn.start()
    pl.semaphore_wait(barrier, 10)

    def send(src, dst, send_sem, recv_sem, device):
        copy = pltpu.make_async_remote_copy(
            src_ref=src, dst_ref=dst, send_sem=send_sem, recv_sem=recv_sem,
            device_id=device, device_id_type=MESH,
        )
        copy.start()
        return copy

    def keep(src, dst, sem):
        copy = pltpu.make_async_copy(src, dst, sem)
        copy.start()
        return copy

    def wait_all(copies):
        for copy in copies:
            copy.wait()

    def fixed(axis, index, ref, columns):
        spot = [slice(None)] * 3
        spot[axis] = index
        return ref.at[(*spot, slice(None), columns)]

    def gather_axis(stage, source, near):
        started = []
        for q, (a, _, _, first, count) in enumerate(OUTBOUND[stage % 2]):
            columns = pl.ds(first, count)
            started.append([
                send(source.at[:, columns], near.at[step, :, columns],
                     sends.at[stage, q, step - 1], recvs.at[stage, q, step - 1], along(a, step))
                for step in (1, 3, 2)
            ])
        return started

    own_rows = [keep(tokens, near1.at[0], out_sem.at[6]), keep(out_grad, near2.at[0], out_sem.at[7])]

    line = lax.broadcasted_iota(jnp.int32, (128, ROWS), 0)
    name = line % 64
    hits = jnp.zeros((128, ROWS), F32)
    weight = jnp.zeros((128, ROWS), F32)
    all_routes, all_gates = routes[...], gates[...].astype(F32)
    for k in range(TOP):
        same = all_routes[k : k + 1] == name
        hits = hits + jnp.where(same, 1.0, 0.0)
        weight = weight + jnp.where(same, all_gates[k : k + 1], 0.0)
    earlier = lax.broadcasted_iota(jnp.int32, (ROWS, ROWS), 0) < lax.broadcasted_iota(
        jnp.int32, (ROWS, ROWS), 1
    )
    rank = dot(hits.astype(BF), jnp.where(earlier, 1.0, 0.0).astype(BF), (1, 0))
    own_info = jnp.where(line < 64, jnp.where(hits > 0.5, rank, 99.0), weight).astype(BF)
    for axis in range(3):
        info[axis, 0] = own_info
    info_copies = [
        [
            send(info.at[axis, 0], info.at[axis, step],
                 info_send.at[axis, step - 1], info_recv.at[axis, step - 1], along(axis, step))
            for step in (1, 3, 2)
        ]
        for axis in range(3)
    ]
    gather1 = gather_axis(0, tokens, near1)
    wait_all(own_rows)

    def pick_masks(number_of, axis, b, c):
        row = lax.broadcasted_iota(jnp.int32, (128, 256), 0)
        column = lax.broadcasted_iota(jnp.int32, (128, 256), 1)
        place = [None, None, None]
        place[axis], place[b], place[c] = me[axis], column // 64, (column // 16) % 4
        expert = 2 * (place[0] * 8 + (place[1] % 2) * 4 + place[2]) + place[1] // 2
        choose_rank = jnp.where(row == expert, 1.0, 0.0).astype(BF)
        choose_gate = jnp.where(row == expert + 64, 1.0, 0.0).astype(BF)
        number = (lax.broadcasted_iota(jnp.int32, (ROWS, 256), 1) % 16).astype(F32)

        def one(step, _):
            ranks = dot(info[axis, step], choose_rank, (0, 0))
            scale = dot(info[axis, step], choose_gate, (0, 0))
            live = ranks == number
            gated[number_of, step] = jnp.where(live, scale, 0.0).astype(BF)
            return 0

        lax.fori_loop(0, 4, one, 0)

    def mask_of(which, step, with_gate):
        mask = gated[which, step]
        return mask if with_gate else jnp.where(mask.astype(F32) != 0.0, 1.0, 0.0).astype(BF)

    def pick(chunk, near, with_gate, picked):
        a, b, c, first, count = chunk
        which = masks[a, b, c]

        def one(step, _):
            rows = dot(mask_of(which, step, with_gate), near[step, :, first : first + count], (0, 0))
            source = (me[a] - step + 4) % 4
            picked[:, :, source, :, first : first + count] = rows.astype(BF).reshape(4, 4, 16, count)
            return 0

        lax.fori_loop(0, 4, one, 0)

    def second_axis(stage, q, picked, onward):
        a, b, _, first, count = OUTBOUND[stage % 2][q]
        columns = pl.ds(first, count)
        landing = (
            onward.at[:, :, me[b], :, columns] if a < b else onward.at[:, me[b], :, :, columns]
        )
        copies = [
            send(picked.at[(me[b] + step) % 4, :, :, :, columns], landing,
                 sends.at[stage, q, step - 1], recvs.at[stage, q, step - 1], along(b, step))
            for step in (1, 3, 2)
        ]
        copies.append(keep(picked.at[me[b], :, :, :, columns], landing, local_sem.at[stage, q]))
        return copies

    def third_axis(stage, q, onward, slots):
        _, _, c, first, count = OUTBOUND[stage % 2][q]
        columns = pl.ds(first, count)
        landing = fixed(c, me[c], slots, columns)
        copies = [
            send(onward.at[(me[c] + step) % 4, :, :, :, columns], landing,
                 sends.at[stage, q, step - 1], recvs.at[stage, q, step - 1], along(c, step))
            for step in (1, 3, 2)
        ]
        copies.append(keep(onward.at[me[c], :, :, :, columns], landing, local_sem.at[stage, q]))
        return copies

    spread1, spread2, final1, final2 = [], [], [], []
    for copies in info_copies:
        wait_all(copies)
    masks = {}
    for axis, b, c in sorted({chunk[:3] for chunk in OUTBOUND[0] + OUTBOUND[1] + INBOUND}):
        masks[axis, b, c] = len(masks)
        pick_masks(masks[axis, b, c], axis, b, c)
    gather2 = gather_axis(1, out_grad, near2)
    for q, chunk in enumerate(OUTBOUND[0]):
        wait_all(gather1[q])
        pick(chunk, near1, False, pick1)
        spread1.append(second_axis(2, q, pick1, fwd1))
    for q, chunk in enumerate(OUTBOUND[1]):
        wait_all(gather2[q])
        pick(chunk, near2, True, pick2)
        spread2.append(second_axis(3, q, pick2, fwd2))
    for q in range(len(OUTBOUND[0])):
        wait_all(spread1[q])
        final1.append(third_axis(4, q, fwd1, slot1))
    for q in range(len(OUTBOUND[1])):
        wait_all(spread2[q])
        final2.append(third_axis(5, q, fwd2, slot2))

    load_gu.wait()
    load_dn.wait()
    for copies in final1:
        wait_all(copies)

    def forward(m, _):
        rows = slot1[m].reshape(256, WIDTH)
        projected = dot(rows, w_gu[...], (1, 0))
        here = pl.ds(pl.multiple_of(m * 256, 256), 256)
        pre_gate = projected[:, :HID]
        pre_up = projected[:, HID:]
        sigmoid_gate = jax.nn.sigmoid(pre_gate)
        activated = pre_gate * sigmoid_gate
        hidden = (activated * pre_up).astype(BF)
        hid[here] = hidden
        by_gate = pre_up * sigmoid_gate * (1.0 + pre_gate * (1.0 - sigmoid_gate))
        pre_grad[here] = jnp.concatenate([by_gate, activated], axis=1).astype(BF)
        pick1[m] = dot(hidden, w_dn[...], (1, 0)).astype(BF).reshape(4, 4, 16, WIDTH)
        return 0

    lax.fori_loop(0, 4, forward, 0)

    def first_back(stage, result, onward):
        started = []
        for q, (_, _, c, first, count) in enumerate(INBOUND):
            columns = pl.ds(first, count)
            landing = onward.at[me[c], :, :, :, columns]
            copies = [
                send(fixed(c, (me[c] + step) % 4, result, columns), landing,
                     sends.at[stage, q, step - 1], recvs.at[stage, q, step - 1], along(c, step))
                for step in (1, 3, 2)
            ]
            copies.append(keep(fixed(c, me[c], result, columns), landing, local_sem.at[stage, q]))
            started.append(copies)
        return started

    def second_back(stage, q, onward, back):
        a, b, _, first, count = INBOUND[q]
        columns = pl.ds(first, count)

        def to(index):
            return onward.at[:, :, index, :, columns] if a < b else onward.at[:, index, :, :, columns]

        landing = back.at[me[b], :, :, :, columns]
        copies = [
            send(to((me[b] + step) % 4), landing,
                 sends.at[stage, q, step - 1], recvs.at[stage, q, step - 1], along(b, step))
            for step in (1, 3, 2)
        ]
        copies.append(keep(to(me[b]), landing, local_sem.at[stage, q]))
        return copies

    def combine(stage, q, back, with_gate, near, part):
        a, b, c, first, count = INBOUND[q]
        which = masks[a, b, c]

        def one(step, _):
            target = (me[a] + step) % 4
            rows = back[:, :, target, :, first : first + count].reshape(256, count)
            near[step, :, first : first + count] = dot(
                mask_of(which, (4 - step) % 4, with_gate), rows, (1, 0)
            ).astype(BF)
            return 0

        lax.fori_loop(0, 4, one, 0)
        columns = pl.ds(first, count)
        return [
            send(near.at[step, :, columns], part.at[step - 1, :, columns],
                 sends.at[stage, q, step - 1], recvs.at[stage, q, step - 1], along(a, step))
            for step in (1, 3, 2)
        ]

    home1 = first_back(6, pick1, bck1)

    for copies in final2:
        wait_all(copies)

    def backward(m, _):
        scaled = slot2[m].reshape(256, WIDTH)
        hidden_grad = dot(scaled, w_dn[...], (1, 1))
        here = pl.ds(pl.multiple_of(m * 256, 256), 256)
        twice = jnp.concatenate([hidden_grad, hidden_grad], axis=1)
        pre_grad[here] = (twice * pre_grad[here].astype(F32)).astype(BF)
        return 0

    def row_gradient(m, _):
        here = pl.ds(pl.multiple_of(m * 256, 256), 256)
        pick2[m] = dot(pre_grad[here], w_gu[...], (1, 1)).astype(BF).reshape(4, 4, 16, WIDTH)
        return 0

    lax.fori_loop(0, 4, backward, 0)

    quarters = [
        pl.multiple_of(QUARTER * (2 * hi + c), QUARTER)
        for c in (1 - core, core)
        for hi in (1 - y_hi, y_hi)
    ]

    def grad_gu(first, t, from_core, w_next):
        here = pl.ds(pl.multiple_of(first + t * 256, 256), 256)
        there = pl.ds(pl.multiple_of(t * 256, 256), 256)
        rows = slot1[:, :, :, :, here].reshape(1024, 256)
        result = dot(rows, pre_grad[...], (0, 0))
        if from_core is not None:
            result = result + core_gu[from_core, there].astype(F32)
        w_next[here] = result.astype(BF)

    def grad_dn(first, t, from_core, w_next):
        here = pl.ds(pl.multiple_of(first + t * 256, 256), 256)
        there = pl.ds(pl.multiple_of(t * 256, 256), 256)
        scaled = slot2[:, :, :, :, here].reshape(1024, 256)
        result = dot(hid[...], scaled, (0, 0))
        if from_core is not None:
            result = result + core_dn[from_core, :, there].astype(F32)
        w_next[:, here] = result.astype(BF)

    def gradients(first, from_core, w_gu_next, w_dn_next):
        def one(t, _):
            grad_gu(first, t, from_core, w_gu_next)
            grad_dn(first, t, from_core, w_dn_next)
            return 0

        lax.fori_loop(0, 2, one, 0)

    pieces = (("gu", 0, 128), ("gu", 128, 128), ("dn", 0, 256), ("gu", 256, 128), ("gu", 384, 128), ("dn", 256, 256))

    def piece_of(p, quarter, mine):
        kind, first, size = pieces[p]
        if kind == "gu":
            return (g_gu if mine else lane_gu), (pl.ds(pl.multiple_of(quarter + first, 128), size),)
        return (w_dn if mine else lane_dn), (slice(None), pl.ds(pl.multiple_of(quarter + first, 128), size))

    across, relocated, stayed = [], [], []

    def send_across(p):
        source, span = piece_of(p, quarters[2], True)
        target, there = piece_of(p, 0, False)
        across.append(send(
            source.at[span], target.at[there], grad_send.at[4 + p], grad_recv.at[4 + p], along(1, 2),
        ))

    moves_own = moving[ex] == y_hi

    def relocate(p):
        across[p].wait()
        held, span = piece_of(p, quarters[3], True)
        lane_held, there = piece_of(p, 0, False)
        mine, theirs = held[span], lane_held[there]
        out_span, stay_span = piece_of(p, quarters[0], True)[1], piece_of(p, quarters[1], True)[1]
        held[out_span] = jnp.where(moves_own, mine, theirs)
        held[stay_span] = jnp.where(moves_own, theirs, mine)
        got, stay = (got_gu, stay_gu) if pieces[p][0] == "gu" else (got_dn, stay_dn)
        relocated.append(send(
            held.at[out_span], got.at[there], grad_send.at[10 + p], grad_recv.at[10 + p], along(0, 2),
        ))
        stayed.append(keep(held.at[stay_span], stay.at[there], out_sem.at[p]))

    to_core, home2, turn1, turn2, last1, last2 = [], [], [], [], [], []

    def gradients_to_core():
        j = len(to_core)
        gradients(quarters[j], None, g_gu, w_dn)
        part_of = pl.ds(quarters[j], QUARTER)
        to_core.append([
            send(g_gu.at[part_of], core_gu.at[j], grad_send.at[2 * j], grad_recv.at[2 * j], other_core),
            send(w_dn.at[:, part_of], core_dn.at[j], grad_send.at[2 * j + 1],
                 grad_recv.at[2 * j + 1], other_core),
        ])

    def gradients_kept(j):
        wait_all(to_core[j])
        gradients(quarters[2 + j], j, g_gu, w_dn)

    def rows_home():
        lax.fori_loop(0, 4, row_gradient, 0)
        home2.extend(first_back(7, pick2, bck2))

    def turn(stage, home, onward, back, turned):
        for q in range(len(INBOUND)):
            wait_all(home[q])
            turned.append(second_back(stage, q, onward, back))

    def finish(stage, turned, back, with_gate, near, part, last):
        for q in range(len(INBOUND)):
            wait_all(turned[q])
            last.append(combine(stage, q, back, with_gate, near, part))

    steps = {
        "rows_home": rows_home,
        "turn1": lambda: turn(8, home1, bck1, back1, turn1),
        "turn2": lambda: turn(9, home2, bck2, back2, turn2),
        "finish1": lambda: finish(10, turn1, back1, True, near1, part1, last1),
        "finish2": lambda: finish(11, turn2, back2, False, near2, part2, last2),
        "to_core": gradients_to_core,
        "kept0": lambda: gradients_kept(0),
        "kept1": lambda: gradients_kept(1),
        "across": lambda: send_across(len(across)),
        "relocate": lambda: relocate(len(relocated)),
    }
    for step in SCHEDULE:
        steps[step]()

    def total(copies, near, part, result, sem):
        for q, (_, _, _, first, count) in enumerate(INBOUND):
            wait_all(copies[q])
            span = slice(first, first + count)
            summed = near[0, :, span].astype(F32)
            for step in range(3):
                summed = summed + part[step, :, span].astype(F32)
            near[0, :, span] = summed.astype(BF)
        return keep(near.at[0], result, out_sem.at[sem])

    stayed.append(total(last1, near1, part1, mixed, 8))
    stayed.append(total(last2, near2, part2, token_grad, 9))
    wait_all(stayed)
    wait_all(relocated)


def place(moving, mixed, token_grad, stay_gu, stay_dn, got_gu, got_dn,
          mixed_out, token_grad_out, gu_out, dn_out, rows_held, gu_held, dn_held, sem_in, sem_out):
    moved = moving[lax.axis_index("expert")]
    moves = [
        (mixed, rows_held.at[0], mixed_out), (token_grad, rows_held.at[1], token_grad_out),
    ]
    for i, (slot, gu, dn) in enumerate(((moved, got_gu, got_dn), (1 - moved, stay_gu, stay_dn))):
        for p in range(2):
            rows = pl.ds(p * 256, 256)
            moves.append((gu.at[rows], gu_held.at[i, rows], gu_out.at[slot, rows]))
        moves.append((dn, dn_held.at[i], dn_out.at[slot]))
    loads = [pltpu.make_async_copy(src, held, sem_in.at[i]) for i, (src, held, _) in enumerate(moves)]
    stores = [pltpu.make_async_copy(held, dst, sem_out.at[i]) for i, (_, held, dst) in enumerate(moves)]
    for copy in loads:
        copy.start()
    for load, store in zip(loads, stores):
        load.wait()
        store.start()
    for copy in stores:
        copy.wait()


def on_device(tokens, routes, gates, out_grad, expert_gate_up, expert_down, moving_slot):
    vmem, anywhere = pl.BlockSpec(memory_space=pltpu.VMEM), pl.BlockSpec(memory_space=pl.ANY)
    slots = (4, 4, 4, CAP, WIDTH)
    sds = jax.ShapeDtypeStruct
    dma = pltpu.SemaphoreType.DMA
    results = pl.pallas_call(
        kernel,
        out_shape=(
            sds((ROWS, WIDTH), BF), sds((ROWS, WIDTH), BF),
            sds((QUARTER, FULL), BF), sds((HID, QUARTER), BF),
            sds((QUARTER, FULL), BF), sds((HID, QUARTER), BF),
            sds(slots, BF), sds(slots, BF), sds(slots, BF), sds(slots, BF),
        ),
        in_specs=[pl.BlockSpec(memory_space=pltpu.SMEM), anywhere, vmem, vmem] + [anywhere] * 3,
        out_specs=(anywhere,) * 10,
        scratch_shapes=[
            pltpu.VMEM((4, ROWS, WIDTH), BF), pltpu.VMEM((4, ROWS, WIDTH), BF),
            pltpu.VMEM(slots, BF), pltpu.VMEM(slots, BF),
            pltpu.VMEM(slots, BF), pltpu.VMEM(slots, BF),
            pltpu.VMEM((WIDTH, FULL), BF), pltpu.VMEM((HID, WIDTH), BF),
            pltpu.VMEM((1024, HID), BF), pltpu.VMEM((1024, FULL), BF),
            pltpu.VMEM(slots, BF), pltpu.VMEM(slots, BF),
            pltpu.VMEM((3, ROWS, WIDTH), BF), pltpu.VMEM((3, ROWS, WIDTH), BF),
            pltpu.VMEM((2, QUARTER, FULL), BF), pltpu.VMEM((2, HID, QUARTER), BF),
            pltpu.VMEM((QUARTER, FULL), BF), pltpu.VMEM((HID, QUARTER), BF),
            pltpu.VMEM((WIDTH, FULL), BF),
            pltpu.VMEM((3, 4, ROWS, 128), BF),
            pltpu.VMEM((MASKS, 4, ROWS, 256), BF),
            dma((12, 6, 3)), dma((12, 6, 3)), dma((3, 3)), dma((3, 3)), dma((12, 6)), dma((2,)),
            dma((16,)), dma((16,)), dma((10,)),
        ],
        compiler_params=pltpu.CompilerParams(
            collective_id=0, has_side_effects=True, vmem_limit_bytes=64 * 2**20 - 2**16
        ),
        cost_estimate=pl.CostEstimate(flops=27 * 10**9, bytes_accessed=40 * 10**6, transcendentals=10**6),
    )(moving_slot, tokens, routes.T, gates.T, out_grad, expert_gate_up, expert_down)
    return pl.pallas_call(
        place,
        out_shape=(
            sds((ROWS, WIDTH), BF), sds((ROWS, WIDTH), BF),
            sds((2, QUARTER, FULL), BF), sds((2, HID, QUARTER), BF),
        ),
        in_specs=[pl.BlockSpec(memory_space=pltpu.SMEM)] + [anywhere] * 6,
        out_specs=(anywhere,) * 4,
        scratch_shapes=[
            pltpu.VMEM((2, ROWS, WIDTH), BF), pltpu.VMEM((2, QUARTER, FULL), BF),
            pltpu.VMEM((2, HID, QUARTER), BF), dma((8,)), dma((8,)),
        ],
    )(moving_slot, *results[:6])


def solution(mesh):
    rows, whole = P(("dp", "expert"), None), P("expert", None, None)
    return jax.shard_map(
        on_device,
        mesh=mesh,
        in_specs=(rows, rows, rows, rows, whole, whole, P()),
        out_specs=(rows, rows, P("expert", "dp", None), P("expert", None, "dp")),
        check_vma=False,
    )
```

time: 235 us -> 222 us (0.945)
  other arithmetic: 5.81 us -> 0 us
  local copies, waits for them, and re-layouts: 5.67 us -> 0 us
    pallas_call x1, Pallas kernels: 222 us -> 214 us  [on_device(): pl.pallas_call(kernel, out_shape=(sds((ROWS, WIDTH), BF), sds((ROWS, WIDT...]
    pallas_call x0 -> x1, Pallas kernels: none -> 5.55 us  [on_device(): pl.pallas_call(place, out_shape=(sds((ROWS, WIDTH), BF), sds((ROWS, WIDTH...]
    select_n x2 -> x0, other arithmetic: 5.16 us -> none  [the longest x1 3.85 us: on_device(): gate_up_grad = jnp.where(moved, got_gu[None], stay_gu[None])]
    unnamed x12 -> x0, local copies, waits for them, and re-layouts: 4.43 us -> none
where the time goes in v2:
time: 222 us; the launch traced here: 221 us
  Pallas kernels  220 us (99%)
    pallas_call x1, Pallas kernels, on_device(): pl.pallas_call(kernel, out_shape=(sds((ROWS, WIDTH), BF), sds((ROWS, WIDT...  214 us
    pallas_call x1, Pallas kernels, on_device(): pl.pallas_call(place, out_shape=(sds((ROWS, WIDTH), BF), sds((ROWS, WIDTH...  5.55 us

profile of v2, /device:TPU:0, one launch (start us, length us, event | category | flops | bytes accessed | tf_op | source)
XLA Modules:
  0.0 220.7 jit_solution(16133582012075299504)
XLA Ops:
  0.6 214.3 %shard_map.102 = (bf16[128,2048]{1,0:T(8,128)(2,1)}, bf16[128,2048]{1,0:T(8,128)(2,1)}, bf16[512,1408]{1,0:T(8,128)(2,1)}, bf16[704,512]{1,0:T(8,128)(2,1)}, bf1...) custom-call(s32[32]{0:T(128)} %moving.3, ...), custom_call_target="tpu_custom_call" | custom-call | flops 27000000512 | bytes 40000000 | tf_op jit(solution)/shard_map/pallas_call | solution.py:458
  215.0 5.6 %shard_map.103 = (bf16[128,2048]{1,0:T(8,128)(2,1)}, bf16[128,2048]{1,0:T(8,128)(2,1)}, bf16[2,512,1408]{2,1,0:T(8,128)(2,1)}, bf16[2,704,512]{2,1,0:T(8,128)(2,1)}) custom-call(s32[32]{0:T(128)} %moving.3, bf16[128,2048]{1,0:T(8,128)(2,1)} %get-tuple-element.10.mixed, bf16[128,2048]{1,0:T(8,128)(2,1)} %get-tuple-element.11.token_grad, ...), custom_call_target="tpu_custom_call" | custom-call | tf_op jit(solution)/shard_map/pallas_call | solution.py:489

commit v3 on v2

--- a/solution.py
+++ b/solution.py
@@ -16,7 +16,7 @@
     ((0, 1, 2, 0, 640), (1, 2, 0, 640, 640), (2, 0, 1, 1280, 768)),
     ((0, 1, 2, 0, 768), (1, 2, 0, 768, 640), (2, 0, 1, 1408, 640)),
 )
-INBOUND = ((0, 1, 2, 0, 768), (1, 2, 0, 768, 768), (2, 0, 1, 1536, 512))
+INBOUND = ((0, 1, 2, 0, 640), (1, 2, 0, 640, 896), (2, 0, 1, 1536, 512))
 
 SCHEDULE = (
     "rows_home", "turn1", "to_core", "to_core", "kept0", "across", "across", "across", "kept1",
@@ -39,7 +39,7 @@
     mixed, token_grad, stay_gu, stay_dn, got_gu, got_dn, fwd1, fwd2, bck1, bck2,
     near1, near2, pick1, pick2, slot1, slot2, w_gu, w_dn, hid, pre_grad,
     back1, back2, part1, part2, core_gu, core_dn, lane_gu, lane_dn, g_gu, info, gated,
-    sends, recvs, info_send, info_recv, local_sem, w_sem, grad_send, grad_recv, out_sem,
+    sends, recvs, info_send, info_recv, w_sem, grad_send, grad_recv, out_sem,
 ):
     dp, ex = lax.axis_index("dp"), lax.axis_index("expert")
     y_hi, core = dp // 2, dp % 2
@@ -81,6 +81,12 @@
         for copy in copies:
             copy.wait()
 
+    def group(sent, received, send_sem, recv_sem):
+        return [
+            pltpu.make_async_copy(received, received, recv_sem),
+            pltpu.make_async_copy(sent, sent, send_sem),
+        ]
+
     def fixed(axis, index, ref, columns):
         spot = [slice(None)] * 3
         spot[axis] = index
@@ -90,11 +96,11 @@
         started = []
         for q, (a, _, _, first, count) in enumerate(OUTBOUND[stage % 2]):
             columns = pl.ds(first, count)
-            started.append([
-                send(source.at[:, columns], near.at[step, :, columns],
-                     sends.at[stage, q, step - 1], recvs.at[stage, q, step - 1], along(a, step))
-                for step in (1, 3, 2)
-            ])
+            sems = sends.at[stage, q], recvs.at[stage, q]
+            for step in (1, 3, 2):
+                send(source.at[:, columns], near.at[step, :, columns], *sems, along(a, step))
+            whole = near.at[pl.ds(1, 3), :, columns]
+            started.append(group(whole, whole, *sems))
         return started
 
     own_rows = [keep(tokens, near1.at[0], out_sem.at[6]), keep(out_grad, near2.at[0], out_sem.at[7])]
@@ -115,14 +121,13 @@
     own_info = jnp.where(line < 64, jnp.where(hits > 0.5, rank, 99.0), weight).astype(BF)
     for axis in range(3):
         info[axis, 0] = own_info
-    info_copies = [
-        [
-            send(info.at[axis, 0], info.at[axis, step],
-                 info_send.at[axis, step - 1], info_recv.at[axis, step - 1], along(axis, step))
-            for step in (1, 3, 2)
-        ]
-        for axis in range(3)
-    ]
+    info_copies = []
+    for axis in range(3):
+        sems = info_send.at[axis], info_recv.at[axis]
+        for step in (1, 3, 2):
+            send(info.at[axis, 0], info.at[axis, step], *sems, along(axis, step))
+        whole = info.at[axis, pl.ds(1, 3)]
+        info_copies.append(group(whole, whole, *sems))
     gather1 = gather_axis(0, tokens, near1)
     wait_all(own_rows)
 
@@ -161,31 +166,32 @@
 
         lax.fori_loop(0, 4, one, 0)
 
+    def quarters_of(buffer, columns, sems):
+        return group(
+            buffer.at[pl.ds(0, 3), :, :, :, columns], buffer.at[:, :, :, :, columns], *sems
+        )
+
     def second_axis(stage, q, picked, onward):
         a, b, _, first, count = OUTBOUND[stage % 2][q]
         columns = pl.ds(first, count)
         landing = (
             onward.at[:, :, me[b], :, columns] if a < b else onward.at[:, me[b], :, :, columns]
         )
-        copies = [
-            send(picked.at[(me[b] + step) % 4, :, :, :, columns], landing,
-                 sends.at[stage, q, step - 1], recvs.at[stage, q, step - 1], along(b, step))
-            for step in (1, 3, 2)
-        ]
-        copies.append(keep(picked.at[me[b], :, :, :, columns], landing, local_sem.at[stage, q]))
-        return copies
+        sems = sends.at[stage, q], recvs.at[stage, q]
+        for step in (1, 3, 2):
+            send(picked.at[(me[b] + step) % 4, :, :, :, columns], landing, *sems, along(b, step))
+        keep(picked.at[me[b], :, :, :, columns], landing, sems[1])
+        return quarters_of(onward, columns, sems)
 
     def third_axis(stage, q, onward, slots):
         _, _, c, first, count = OUTBOUND[stage % 2][q]
         columns = pl.ds(first, count)
         landing = fixed(c, me[c], slots, columns)
-        copies = [
-            send(onward.at[(me[c] + step) % 4, :, :, :, columns], landing,
-                 sends.at[stage, q, step - 1], recvs.at[stage, q, step - 1], along(c, step))
-            for step in (1, 3, 2)
-        ]
-        copies.append(keep(onward.at[me[c], :, :, :, columns], landing, local_sem.at[stage, q]))
-        return copies
+        sems = sends.at[stage, q], recvs.at[stage, q]
+        for step in (1, 3, 2):
+            send(onward.at[(me[c] + step) % 4, :, :, :, columns], landing, *sems, along(c, step))
+        keep(onward.at[me[c], :, :, :, columns], landing, sems[1])
+        return quarters_of(slots, columns, sems)
 
     spread1, spread2, final1, final2 = [], [], [], []
     for copies in info_copies:
@@ -237,13 +243,11 @@
         for q, (_, _, c, first, count) in enumerate(INBOUND):
             columns = pl.ds(first, count)
             landing = onward.at[me[c], :, :, :, columns]
-            copies = [
-                send(fixed(c, (me[c] + step) % 4, result, columns), landing,
-                     sends.at[stage, q, step - 1], recvs.at[stage, q, step - 1], along(c, step))
-                for step in (1, 3, 2)
-            ]
-            copies.append(keep(fixed(c, me[c], result, columns), landing, local_sem.at[stage, q]))
-            started.append(copies)
+            sems = sends.at[stage, q], recvs.at[stage, q]
+            for step in (1, 3, 2):
+                send(fixed(c, (me[c] + step) % 4, result, columns), landing, *sems, along(c, step))
+            keep(fixed(c, me[c], result, columns), landing, sems[1])
+            started.append(quarters_of(onward, columns, sems))
         return started
 
     def second_back(stage, q, onward, back):
@@ -254,13 +258,11 @@
             return onward.at[:, :, index, :, columns] if a < b else onward.at[:, index, :, :, columns]
 
         landing = back.at[me[b], :, :, :, columns]
-        copies = [
-            send(to((me[b] + step) % 4), landing,
-                 sends.at[stage, q, step - 1], recvs.at[stage, q, step - 1], along(b, step))
-            for step in (1, 3, 2)
-        ]
-        copies.append(keep(to(me[b]), landing, local_sem.at[stage, q]))
-        return copies
+        sems = sends.at[stage, q], recvs.at[stage, q]
+        for step in (1, 3, 2):
+            send(to((me[b] + step) % 4), landing, *sems, along(b, step))
+        keep(to(me[b]), landing, sems[1])
+        return quarters_of(back, columns, sems)
 
     def combine(stage, q, back, with_gate, near, part):
         a, b, c, first, count = INBOUND[q]
@@ -276,11 +278,11 @@
 
         lax.fori_loop(0, 4, one, 0)
         columns = pl.ds(first, count)
-        return [
-            send(near.at[step, :, columns], part.at[step - 1, :, columns],
-                 sends.at[stage, q, step - 1], recvs.at[stage, q, step - 1], along(a, step))
-            for step in (1, 3, 2)
-        ]
+        sems = sends.at[stage, q], recvs.at[stage, q]
+        for step in (1, 3, 2):
+            send(near.at[step, :, columns], part.at[step - 1, :, columns], *sems, along(a, step))
+        whole = part.at[:, :, columns]
+        return group(whole, whole, *sems)
 
     home1 = first_back(6, pick1, bck1)
 
@@ -339,7 +341,7 @@
     def piece_of(p, quarter, mine):
         kind, first, size = pieces[p]
         if kind == "gu":
-            return (g_gu if mine else lane_gu), (pl.ds(pl.multiple_of(quarter + first, 128), size),)
+            return (g_gu if mine else lane_gu), (pl.ds(pl.multiple_of(quarter + first, 64), size),)
         return (w_dn if mine else lane_dn), (slice(None), pl.ds(pl.multiple_of(quarter + first, 128), size))
 
     across, relocated, stayed = [], [], []
@@ -478,7 +480,7 @@
             pltpu.VMEM((WIDTH, FULL), BF),
             pltpu.VMEM((3, 4, ROWS, 128), BF),
             pltpu.VMEM((MASKS, 4, ROWS, 256), BF),
-            dma((12, 6, 3)), dma((12, 6, 3)), dma((3, 3)), dma((3, 3)), dma((12, 6)), dma((2,)),
+            dma((12, 3)), dma((12, 3)), dma((3,)), dma((3,)), dma((2,)),
             dma((16,)), dma((16,)), dma((10,)),
         ],
         compiler_params=pltpu.CompilerParams(

time: 222 us -> 216 us (0.973)
  Pallas kernels: 220 us -> 215 us
    pallas_call x1, Pallas kernels: 214 us -> 210 us  [on_device(): pl.pallas_call(kernel, out_shape=(sds((ROWS, WIDTH), BF), sds((ROWS, WIDT...]
where the time goes in v3:
time: 216 us
  Pallas kernels  215 us (100%)
    pallas_call x1, Pallas kernels, on_device(): pl.pallas_call(kernel, out_shape=(sds((ROWS, WIDTH), BF), sds((ROWS, WIDT...  210 us
    pallas_call x1, Pallas kernels, on_device(): pl.pallas_call(place, out_shape=(sds((ROWS, WIDTH), BF), sds((ROWS, WIDTH...  5.55 us

profile of v3, /device:TPU:0, one launch (start us, length us, event | category | flops | bytes accessed | tf_op | source)
XLA Modules:
  0.0 215.9 jit_solution(10493525116642088138)
XLA Ops:
  0.6 209.7 %shard_map.102 = (bf16[128,2048]{1,0:T(8,128)(2,1)}, bf16[128,2048]{1,0:T(8,128)(2,1)}, bf16[512,1408]{1,0:T(8,128)(2,1)}, bf16[704,512]{1,0:T(8,128)(2,1)}, bf1...) custom-call(s32[32]{0:T(128)} %moving.3, ...), custom_call_target="tpu_custom_call" | custom-call | flops 27000000512 | bytes 40000000 | tf_op jit(solution)/shard_map/pallas_call | solution.py:460
  210.4 5.6 %shard_map.103 = (bf16[128,2048]{1,0:T(8,128)(2,1)}, bf16[128,2048]{1,0:T(8,128)(2,1)}, bf16[2,512,1408]{2,1,0:T(8,128)(2,1)}, bf16[2,704,512]{2,1,0:T(8,128)(2,1)}) custom-call(s32[32]{0:T(128)} %moving.3, bf16[128,2048]{1,0:T(8,128)(2,1)} %get-tuple-element.10.mixed, bf16[128,2048]{1,0:T(8,128)(2,1)} %get-tuple-element.11.token_grad, ...), custom_call_target="tpu_custom_call" | custom-call | tf_op jit(solution)/shard_map/pallas_call | solution.py:491

commit v4 on v3

--- a/solution.py
+++ b/solution.py
@@ -62,7 +62,6 @@
     load_dn = pltpu.make_async_copy(down.at[y_hi], w_dn, w_sem.at[1])
     load_gu.start()
     load_dn.start()
-    pl.semaphore_wait(barrier, 10)
 
     def send(src, dst, send_sem, recv_sem, device):
         copy = pltpu.make_async_remote_copy(
@@ -121,6 +120,7 @@
     own_info = jnp.where(line < 64, jnp.where(hits > 0.5, rank, 99.0), weight).astype(BF)
     for axis in range(3):
         info[axis, 0] = own_info
+    pl.semaphore_wait(barrier, 10)
     info_copies = []
     for axis in range(3):
         sems = info_send.at[axis], info_recv.at[axis]

time: 216 us -> 216 us (level)
  no operation moved by 1% of the time
where the time goes in v4:
time: 216 us
  Pallas kernels  215 us (100%)
    pallas_call x1, Pallas kernels, on_device(): pl.pallas_call(kernel, out_shape=(sds((ROWS, WIDTH), BF), sds((ROWS, WIDT...  210 us
    pallas_call x1, Pallas kernels, on_device(): pl.pallas_call(place, out_shape=(sds((ROWS, WIDTH), BF), sds((ROWS, WIDTH...  5.55 us

profile of v4, /device:TPU:0, one launch (start us, length us, event | category | flops | bytes accessed | tf_op | source)
XLA Modules:
  0.0 215.7 jit_solution(2602210573494758917)
XLA Ops:
  0.6 209.5 %shard_map.102 = (bf16[128,2048]{1,0:T(8,128)(2,1)}, bf16[128,2048]{1,0:T(8,128)(2,1)}, bf16[512,1408]{1,0:T(8,128)(2,1)}, bf16[704,512]{1,0:T(8,128)(2,1)}, bf1...) custom-call(s32[32]{0:T(128)} %moving.3, ...), custom_call_target="tpu_custom_call" | custom-call | flops 27000000512 | bytes 40000000 | tf_op jit(solution)/shard_map/pallas_call | solution.py:460
  210.2 5.6 %shard_map.103 = (bf16[128,2048]{1,0:T(8,128)(2,1)}, bf16[128,2048]{1,0:T(8,128)(2,1)}, bf16[2,512,1408]{2,1,0:T(8,128)(2,1)}, bf16[2,704,512]{2,1,0:T(8,128)(2,1)}) custom-call(s32[32]{0:T(128)} %moving.3, bf16[128,2048]{1,0:T(8,128)(2,1)} %get-tuple-element.10.mixed, bf16[128,2048]{1,0:T(8,128)(2,1)} %get-tuple-element.11.token_grad, ...), custom_call_target="tpu_custom_call" | custom-call | tf_op jit(solution)/shard_map/pallas_call | solution.py:491
